TPU v7x, 256 devices: a whole 4x4x8 slice. The times are simulated.
256 devices in a mesh: blk: 16 (over z, core), cube: 16 (over y, x).
Axes of the slice: x: 4, y: 4, z: 8, core: 2. Of those that a mesh axis runs over, the one named last changes fastest.
Arguments:
- activations: bfloat16 [131072, 8192], P(('blk', 'cube')), may hold values from -16 to 16, as said below
- out_grads: bfloat16 [131072, 512], P(('blk', 'cube')), may hold values from -1 to 1, as said below
Outputs:
- combined: float32 [8192, 512], P('blk', 'cube')
Inputs may be any that keep to these rules, and one draw needn't show every extreme that they name: Real-valued activations. `out_grads`: Real-valued output gradients.
All inputs are finite; a program needn't handle non-finite values.
Results may differ from a plain program's by a relative error of at most 0.0003.
Values may be sent and summed in bfloat16 or wider, within the bound.
A program may use at most 128 MiB of HBM per device.

v0:
```python
import jax
import jax.numpy as jnp
from jax import lax
from jax.sharding import PartitionSpec as P

epsilon = 1e-06


def partner_2(x, axis, bit):
    return lax.ppermute(x, axis, [(i, i ^ 1 << bit) for i in range(lax.axis_size(axis))])


def shards(activations, out_grads):
    shard_grad = lax.psum_scatter(
        lax.dot_general(
            activations, out_grads, (((0,), (0,)), ((), ())), preferred_element_type=jnp.float32
        ),
        "blk",
        scatter_dimension=0,
        tiled=True,
    )
    group_id = lax.axis_index("cube")
    group_total = lax.axis_size("cube")
    levels_total = group_total.bit_length() - 1
    for bit_level in range(levels_total):
        partner = partner_2(shard_grad, "cube", bit_level)
        is_upper = group_id // 2**bit_level % 2 == 1
        former = jnp.where(is_upper, partner, shard_grad)
        latter = jnp.where(is_upper, shard_grad, partner)
        inner_prod, former_sq, latter_sq = lax.psum(
            (jnp.sum(former * latter), jnp.sum(former * former), jnp.sum(latter * latter)), "blk"
        )
        shard_grad = (1.0 - inner_prod / (2.0 * (former_sq + epsilon))) * former + (
            1.0 - inner_prod / (2.0 * (latter_sq + epsilon))
        ) * latter
    col_width = shard_grad.shape[1] // group_total
    return lax.dynamic_slice_in_dim(shard_grad, group_id * col_width, col_width, 1)


def solution(mesh):
    placed = (P(("blk", "cube"), None), P(("blk", "cube"), None))
    return jax.shard_map(
        shards, mesh=mesh, in_specs=placed, out_specs=P("blk", "cube"), check_vma=False
    )
```

profile of v0, /device:TPU:1, one launch (start us, length us, event | category | flops | bytes accessed | tf_op | source)
XLA Modules:
  0.0 359.2 jit_solution(14622062818969824526)
XLA Ops:
  6.5 0.0 copy-start
  6.5 0.0 reduce-scatter.2.cloned.1.call-start
  6.5 1.0 copy-done
  7.6 11.7 %fusion.1 = f32[8192,512]{1,0:T(8,128)} fusion(bf16[512,8192]{1,0:T(8,128)(2,1)} %param.2, bf16[512,512]{1,0:T(8,128)(2,1)S(1)} %copy-done), kind=kOutput, calls=%fused_computation.26 | convolution fusion | flops 4294967296 | bytes 25690112 | tf_op jit(solution)/shard_map/dot_general | solution.py:15
  19.2 0.0 reduce-scatter.2.cloned.1.call-update
  19.3 103.4 %reduce-scatter.2.cloned.1.call-done = f32[512,512]{1,0:T(8,128)} async-done(((f32[8192,512]{1,0:T(8,128)}), f32[512,512]{1,0:T(8,128)}) %reduce-scatter.2.cloned.1.call-update) | async-done | bytes 1048592 | tf_op jit(solution)/shard_map/reduce_scatter | solution.py:14
  122.7 1.2 collective-permute-start
  123.8 21.9 %collective-permute-done = f32[512,512]{1,0:T(8,128)S(1)} collective-permute-done((f32[512,512]{1,0:T(8,128)}, f32[512,512]{1,0:T(8,128)S(1)}, u32[]{:S(2)}, u32[]{:S(2)}) %collective-permute-start) | collective-permute-done | bytes 1048608 | tf_op jit(solution)/shard_map/ppermute | solution.py:10
  145.8 3.2 multiply_reduce_fusion.10
  148.9 26.3 %all-reduce.3 = (f32[]{:T(128)}, f32[]{:T(128)}, f32[]{:T(128)}) all-reduce(f32[]{:T(128)} %get-tuple-element.15, f32[]{:T(128)} %get-tuple-element.16, f32[]{:T(128)} %get-tuple-element.14), channel_id=1, replica_groups=mesh['blk'=16,'cube'=16] {'blk'}, use_global_device_ids=true, to_apply=%region_2.3 | all-reduce | flops 3 | bytes 24 | tf_op jit(solution)/shard_map/psum | solution.py:30
  177.8 1.5 multiply_add_fusion.2
  179.2 2.8 collective-permute-start.1
  182.0 22.1 %collective-permute-done.1 = f32[512,512]{1,0:T(8,128)} collective-permute-done((f32[512,512]{1,0:T(8,128)S(1)}, f32[512,512]{1,0:T(8,128)}, u32[]{:S(2)}, u32[]{:S(2)}) %collective-permute-start.1) | collective-permute-done | bytes 1048608 | tf_op jit(solution)/shard_map/ppermute | solution.py:10
  204.1 3.1 multiply_reduce_fusion.7
  207.3 25.9 %all-reduce.2 = (f32[]{:T(128)}, f32[]{:T(128)}, f32[]{:T(128)}) all-reduce(f32[]{:T(128)} %get-tuple-element.12, f32[]{:T(128)} %get-tuple-element.13, f32[]{:T(128)} %get-tuple-element.11), channel_id=1, replica_groups=mesh['blk'=16,'cube'=16] {'blk'}, use_global_device_ids=true, to_apply=%region_8.9 | all-reduce | flops 3 | bytes 24 | tf_op jit(solution)/shard_map/psum | solution.py:30
  235.8 1.5 multiply_add_fusion.1
  237.3 1.3 collective-permute-start.2
  238.6 23.0 %collective-permute-done.2 = f32[512,512]{1,0:T(8,128)} collective-permute-done((f32[512,512]{1,0:T(8,128)S(1)}, f32[512,512]{1,0:T(8,128)}, u32[]{:S(2)}, u32[]{:S(2)}) %collective-permute-start.2) | collective-permute-done | bytes 1048608 | tf_op jit(solution)/shard_map/ppermute | solution.py:10
  261.5 3.1 multiply_reduce_fusion.4
  264.6 25.1 %all-reduce.1 = (f32[]{:T(128)}, f32[]{:T(128)}, f32[]{:T(128)}) all-reduce(f32[]{:T(128)} %get-tuple-element.9, f32[]{:T(128)} %get-tuple-element.10, f32[]{:T(128)} %get-tuple-element.8), channel_id=1, replica_groups=mesh['blk'=16,'cube'=16] {'blk'}, use_global_device_ids=true, to_apply=%region_14.15 | all-reduce | flops 3 | bytes 24 | tf_op jit(solution)/shard_map/psum | solution.py:30
  292.4 1.5 multiply_add_fusion
  293.8 2.8 collective-permute-start.3
  296.6 22.9 %collective-permute-done.3 = f32[512,512]{1,0:T(8,128)} collective-permute-done((f32[512,512]{1,0:T(8,128)S(1)}, f32[512,512]{1,0:T(8,128)}, u32[]{:S(2)}, u32[]{:S(2)}) %collective-permute-start.3) | collective-permute-done | bytes 1048608 | tf_op jit(solution)/shard_map/ppermute | solution.py:10
  319.6 3.1 multiply_reduce_fusion.1
  322.7 25.1 %all-reduce = (f32[]{:T(128)}, f32[]{:T(128)}, f32[]{:T(128)}) all-reduce(f32[]{:T(128)} %get-tuple-element.6, f32[]{:T(128)} %get-tuple-element.7, f32[]{:T(128)} %get-tuple-element.5), channel_id=1, replica_groups=mesh['blk'=16,'cube'=16] {'blk'}, use_global_device_ids=true, to_apply=%region_20.21 | all-reduce | flops 3 | bytes 24 | tf_op jit(solution)/shard_map/psum | solution.py:30
  350.4 1.2 fusion
  351.6 0.7 copy.3
Async XLA Ops:
  6.5 1.0 copy-start
  6.5 116.1 %reduce-scatter.2.cloned.1.call-start = ((), (), s32[]{:S(2)}) async-start(), calls=%async_computation.1 | async-start | bytes 17825792 | tf_op jit(solution)/shard_map/reduce_scatter | solution.py:14
  122.7 23.1 %collective-permute-start = (f32[512,512]{1,0:T(8,128)}, f32[512,512]{1,0:T(8,128)S(1)}, u32[]{:S(2)}, u32[]{:S(2)}) collective-permute-start(f32[512,512]{1,0:T(8,128)} %reduce-scatter.2.cloned.1.call-done), channel_id=1, source_target_pairs={{0,1},{1,0},{2,3},{3,2},{4,5},{5,4},{6,7},{7,6},{8,9},{9,8},{10,11... | collective-permute-start | bytes 3145736 | tf_op jit(solution)/shard_map/ppermute | solution.py:10
  179.2 24.9 %collective-permute-start.1 = (f32[512,512]{1,0:T(8,128)S(1)}, f32[512,512]{1,0:T(8,128)}, u32[]{:S(2)}, u32[]{:S(2)}) collective-permute-start(f32[512,512]{1,0:T(8,128)S(1)} %multiply_add_fusion.2), channel_id=1, source_target_pairs={{0,2},{1,3},{2,0},{3,1},{4,6},{5,7},{6,4},{7,5},{8,10},{9,11},{10,... | collective-permute-start | bytes 3145736 | tf_op jit(solution)/shard_map/ppermute | solution.py:10
  237.3 24.3 %collective-permute-start.2 = (f32[512,512]{1,0:T(8,128)S(1)}, f32[512,512]{1,0:T(8,128)}, u32[]{:S(2)}, u32[]{:S(2)}) collective-permute-start(f32[512,512]{1,0:T(8,128)S(1)} %multiply_add_fusion.1), channel_id=1, source_target_pairs={{0,4},{1,5},{2,6},{3,7},{4,0},{5,1},{6,2},{7,3},{8,12},{9,13},{10,... | collective-permute-start | bytes 3145736 | tf_op jit(solution)/shard_map/ppermute | solution.py:10
  293.8 25.8 %collective-permute-start.3 = (f32[512,512]{1,0:T(8,128)S(1)}, f32[512,512]{1,0:T(8,128)}, u32[]{:S(2)}, u32[]{:S(2)}) collective-permute-start(f32[512,512]{1,0:T(8,128)S(1)} %multiply_add_fusion), channel_id=1, source_target_pairs={{0,8},{1,9},{2,10},{3,11},{4,12},{5,13},{6,14},{7,15},{8,0},{9,1},... | collective-permute-start | bytes 3145736 | tf_op jit(solution)/shard_map/ppermute | solution.py:10
Sparse Core Ops, SparseCore 0:
  19.4 103.2 reduce-scatter.1
where the time goes:
time: 360 us; the launch traced here: 359 us
  waiting for transfers between devices  193 us (54%)
  blocking collectives  102 us (28%)
  between operations  23.8 us (7%)
  other arithmetic  18.1 us (5%)
  matrix products  11.7 us (3%)
  starting transfers between devices  8.08 us (2%)
    reduce_scatter x1, waiting for transfers between devices, shards(): lax.psum_scatter(lax.dot_general(activations, out_grads, (((0,), (0,)), (...  103 us
    psum x4, blocking collectives, shards(): lax.psum((jnp.sum(former * latter), jnp.sum(former * former), jnp.sum(lat...  102 us
    ppermute x4, waiting for transfers between devices, partner_2(): lax.ppermute(x, axis, [(i, i ^ 1 << bit) for i in range(lax.axis_size(axi...  90 us
    reduce_sum x4, other arithmetic, shards(): jnp.sum(former * former)  12.5 us
    dot_general x1, matrix products, shards(): lax.dot_general(activations, out_grads, (((0,), (0,)), ((), ())), preferr...  11.7 us
    ppermute x4, starting transfers between devices, partner_2(): lax.ppermute(x, axis, [(i, i ^ 1 << bit) for i in range(lax.axis_size(axi...  8.08 us
  transfers between devices with their start and end apart: 5, of which 5 were waited for; matrix products, arithmetic and copies ran while one was open for 0% of the time, Pallas kernels for 0%

commit v1 on v0

v1 whole, which is shorter than its diff:
```python
import jax
import jax.numpy as jnp
from jax import lax
from jax.experimental import pallas as pl
from jax.experimental.pallas import tpu as pltpu
from jax.sharding import PartitionSpec as P

MESH = pl.DeviceIdType.MESH
EPS = 1e-6
NZ = 8
NG = 16
STEPS = NZ - 1
F32, BF16 = jnp.float32, jnp.bfloat16
SLOTS = (7, 1, 6, 2, 5, 3, 4, 0)


def kernel(
    a_hbm, g_hbm, out_ref,
    av, gv, gt, hs, hr, ls, lr, xs, xr, zs, zr, ks, kz, kc,
    own_sem, par_send, par_recv, hi_send, hi_recv, lo_send, lo_recv,
    x_send, x_recv, z_send, z_recv, k_send, k_recv,
):
    b = lax.axis_index("blk")
    g = lax.axis_index("cube")
    z, core = b >> 1, b & 1
    y, x = g >> 2, g & 3
    partner = (b ^ 1, g)
    ring = (
        (((z + 1) & 7) * 2 + core, g),
        (((z + 7) & 7) * 2 + core, g),
    )
    plane = []
    for k in range(1, NG):
        plane.append((((y + k // 4) & 3) * 4) + ((x + k % 4) & 3))
    line = [b ^ j for j in range(1, NG)]
    tok = a_hbm.shape[0]
    bw = a_hbm.shape[1] // (2 * NZ)
    half = bw // 2
    kv = g_hbm.shape[1]
    kvh = kv // 2
    ks_rows = kv // NG

    barrier = pltpu.get_barrier_semaphore()
    for p in line:
        pl.semaphore_signal(barrier, inc=1, device_id=(p, g), device_id_type=MESH)
    for p in plane:
        pl.semaphore_signal(barrier, inc=1, device_id=(b, p), device_id_type=MESH)

    def block(slot, parity):
        start = (((z + slot) & 7) * 2 + parity) * bw
        return a_hbm.at[:, pl.ds(pl.multiple_of(start, bw), bw)]

    own = [pltpu.make_async_copy(g_hbm, gv.at[pl.ds(0, tok)], own_sem.at[NZ])]
    own[0].start()
    for s in range(NZ):
        own.append(pltpu.make_async_copy(block(s, core), av.at[s, pl.ds(0, tok)], own_sem.at[s]))
    for s in SLOTS:
        own[s + 1].start()

    pl.semaphore_wait(barrier, 2 * (NG - 1))

    def remote(src, dst, send, recv, dev):
        return pltpu.make_async_remote_copy(
            src_ref=src, dst_ref=dst, send_sem=send, recv_sem=recv, device_id=dev, device_id_type=MESH
        )

    par = [remote(g_hbm, gv.at[pl.ds(tok, tok)], par_send.at[NZ], par_recv.at[NZ], partner)]
    par[0].start()
    for s in range(NZ):
        par.append(
            remote(block(s, 1 - core), av.at[s, pl.ds(tok, tok)], par_send.at[s], par_recv.at[s], partner)
        )
    for s in SLOTS:
        par[s + 1].start()

    own[0].wait()
    gt[:, :tok] = gv[:tok, :].T
    par[0].wait_recv()
    gt[:, tok:] = gv[tok:, :].T

    waited = set()

    def ready(slot):
        if slot not in waited:
            waited.add(slot)
            own[slot + 1].wait()
            par[slot + 1].wait_recv()

    def share(slot, way, h):
        return jnp.dot(
            gt[way * kvh : (way + 1) * kvh, :],
            av[slot, :, h * half : (h + 1) * half],
            preferred_element_type=F32,
        )

    def hop(t, way, h):
        return remote(hs.at[t, way, h], hr.at[t, way, h], hi_send.at[t, way, h], hi_recv.at[t, way, h], ring[way])

    def spread(src, dst, send, recv):
        for p in plane:
            remote(src.at[p], dst.at[g], send, recv, (b, p)).start()
        pltpu.make_async_copy(src.at[g], dst.at[g], recv).start()

    def spread_wait_recv(dst, recv):
        pltpu.make_async_copy(dst, dst, recv).wait()

    def spread_wait_send(src, send):
        part = src.at[pl.ds(0, NG - 1)]
        pltpu.make_async_copy(part, part, send).wait()

    for t in range(STEPS + 1):
        for h in range(2):
            for way in range(2):
                if t == STEPS:
                    slot = 0
                else:
                    slot = NZ - 1 - t if way == 0 else 1 + t
                ready(slot)
                total = share(slot, way, h)
                if t > 0:
                    hop(t - 1, way, h).wait_recv()
                    total = total + hr[t - 1, way, h].astype(F32)
                hi = total.astype(BF16)
                if t < STEPS:
                    hs[t, way, h] = hi
                    hop(t, way, h).start()
                else:
                    xs[h, way * 8 : way * 8 + 8] = hi.reshape(8, ks_rows, half)
                lo = (total - hi.astype(F32)).astype(BF16)
                ls[t, way * 8 : way * 8 + 8, :, h * half : (h + 1) * half] = lo.reshape(8, ks_rows, half)
            if t == STEPS:
                spread(xs.at[h], xr.at[h], x_send.at[h], x_recv.at[h])
        spread(ls.at[t], lr.at[t], lo_send.at[t], lo_recv.at[t])

    gram = None
    for h in range(2):
        spread_wait_recv(xr.at[h], x_recv.at[h])
        rows = xr[h].reshape(kv, half)
        part = lax.dot_general(rows, rows, (((1,), (1,)), ((), ())), preferred_element_type=F32)
        gram = part if gram is None else gram + part
    same = (lax.broadcasted_iota(jnp.int32, (kv, kv), 0) & (ks_rows - 1)) == (
        lax.broadcasted_iota(jnp.int32, (kv, kv), 1) & (ks_rows - 1)
    )
    gram = jnp.where(same, gram, 0.0).reshape(NG, ks_rows, kv).sum(axis=1)
    pick = (lax.broadcasted_iota(jnp.int32, (kv, 128), 0) >> 5) == lax.broadcasted_iota(jnp.int32, (kv, 128), 1)
    gram = jnp.dot(gram, pick.astype(F32), precision=lax.Precision.HIGHEST, preferred_element_type=F32)

    ks[0] = gram
    kz[b] = gram
    for p in line:
        remote(ks.at[0], kz.at[b], k_send.at[0], k_recv.at[0], (p, g)).start()
    most = pl.ds(0, NG - 1)
    pltpu.make_async_copy(kz.at[most], kz.at[most], k_recv.at[0]).wait()
    gram = kz[...].sum(axis=0)
    ks[1] = gram
    kc[g] = gram
    for p in plane:
        remote(ks.at[1], kc.at[g], k_send.at[1], k_recv.at[1], (b, p)).start()
    pltpu.make_async_copy(kc.at[most], kc.at[most], k_recv.at[1]).wait()
    gram = kc[...].sum(axis=0)

    row = lax.broadcasted_iota(jnp.int32, (NG, 128), 0)
    col = lax.broadcasted_iota(jnp.int32, (NG, 128), 1)
    coef = jnp.ones((NG, 1), F32)
    for level in range(4):
        bit = 1 << level
        diag = jnp.where(row == col, gram, 0.0)
        cross = jnp.where((row ^ bit) == col, gram, 0.0)

        def factor(axis):
            sq = jnp.maximum(jnp.sum(diag, axis=axis, keepdims=True), 0.0)
            return 1.0 - jnp.sum(cross, axis=axis, keepdims=True) / (2.0 * (sq + EPS))

        by_row, by_col = factor(1), factor(0)
        coef = coef * by_row
        gram = gram * by_row * by_col
        gram = gram + jnp.where((row & bit) != 0, pltpu.roll(gram, bit, 0), pltpu.roll(gram, NG - bit, 0))
        gram = gram + jnp.where((col & bit) != 0, pltpu.roll(gram, bit, 1), pltpu.roll(gram, 128 - bit, 1))
    coef = jnp.broadcast_to(coef, (NG, 128))

    def combine(ref):
        width = ref.shape[-1]
        acc = jnp.zeros((ks_rows, width), F32)
        for i in range(NG):
            acc = acc + jnp.tile(coef[i : i + 1], (1, width // 128)) * ref[i].astype(F32)
        return acc

    side = 2 * (g >> 3) - 1
    home = []
    for t in range(STEPS):
        spread_wait_recv(lr.at[t], lo_recv.at[t])
        zs[t] = combine(lr.at[t]).astype(BF16)
        dest = (z + (1 + t) * side + 8) & 7
        home.append(remote(zs.at[t], zr.at[t], z_send.at[t], z_recv.at[t], (dest * 2 + core, g)))
        home[t].start()
    spread_wait_recv(lr.at[STEPS], lo_recv.at[STEPS])
    acc = combine(lr.at[STEPS])
    acc = acc + jnp.concatenate([combine(xr.at[0]), combine(xr.at[1])], axis=1)
    for t in range(STEPS):
        home[t].wait_recv()
        acc = acc + zr[t].astype(F32)
    out_ref[...] = acc

    for s in range(NZ + 1):
        par[s].wait_send()
    for t in range(STEPS):
        home[t].wait_send()
        for way in range(2):
            for h in range(2):
                hop(t, way, h).wait_send()
    for t in range(STEPS + 1):
        spread_wait_send(ls.at[t], lo_send.at[t])
    for h in range(2):
        spread_wait_send(xs.at[h], x_send.at[h])
    for s in range(2):
        pltpu.make_async_copy(kz.at[most], kz.at[most], k_send.at[s]).wait()


def shards(activations, out_grads):
    tok, d = activations.shape
    kv = out_grads.shape[1]
    bw = d // (2 * NZ)
    half = bw // 2
    rows = kv // NG
    dma = pltpu.SemaphoreType.DMA
    grad = pl.pallas_call(
        kernel,
        out_shape=jax.ShapeDtypeStruct((rows, bw), F32),
        in_specs=[pl.BlockSpec(memory_space=pl.ANY)] * 2,
        out_specs=pl.BlockSpec(memory_space=pltpu.VMEM),
        scratch_shapes=[
            pltpu.VMEM((NZ, 2 * tok, bw), BF16),
            pltpu.VMEM((2 * tok, kv), BF16),
            pltpu.VMEM((kv, 2 * tok), BF16),
            pltpu.VMEM((STEPS, 2, 2, kv // 2, half), BF16),
            pltpu.VMEM((STEPS, 2, 2, kv // 2, half), BF16),
            pltpu.VMEM((NZ, NG, rows, bw), BF16),
            pltpu.VMEM((NZ, NG, rows, bw), BF16),
            pltpu.VMEM((2, NG, rows, half), BF16),
            pltpu.VMEM((2, NG, rows, half), BF16),
            pltpu.VMEM((STEPS, rows, bw), BF16),
            pltpu.VMEM((STEPS, rows, bw), BF16),
            pltpu.VMEM((2, NG, 128), F32),
            pltpu.VMEM((NG, NG, 128), F32),
            pltpu.VMEM((NG, NG, 128), F32),
            dma((NZ + 1,)),
            dma((NZ + 1,)),
            dma((NZ + 1,)),
            dma((STEPS, 2, 2)),
            dma((STEPS, 2, 2)),
            dma((NZ,)),
            dma((NZ,)),
            dma((2,)),
            dma((2,)),
            dma((STEPS,)),
            dma((STEPS,)),
            dma((2,)),
            dma((2,)),
        ],
        compiler_params=pltpu.CompilerParams(
            collective_id=0, has_side_effects=True, vmem_limit_bytes=56 << 20
        ),
        cost_estimate=pl.CostEstimate(
            flops=2 * tok * d * kv, bytes_accessed=2 * tok * (d + kv), transcendentals=0
        ),
        name="adasum",
    )(activations, out_grads)
    return grad.T


def solution(mesh):
    placed = (P(("blk", "cube"), None), P(("blk", "cube"), None))
    return jax.shard_map(
        shards, mesh=mesh, in_specs=placed, out_specs=P("blk", "cube"), check_vma=False
    )
```

time: 360 us -> 91.8 us (0.26)
  waiting for transfers between devices: 193 us -> 0 us
  blocking collectives: 102 us -> 0 us
  Pallas kernels: 0 us -> 90.2 us
  between operations: 23.8 us -> 0.01 us
  other arithmetic: 18.1 us -> 0 us
  matrix products: 11.7 us -> 0 us
  starting transfers between devices: 8.08 us -> 0 us
    reduce_scatter x1 -> x0, waiting for transfers between devices: 103 us -> none  [shards(): lax.psum_scatter(lax.dot_general(activations, out_grads, (((0,), (0,)), (...]
    psum x4 -> x0, blocking collectives: 102 us -> none  [shards(): lax.psum((jnp.sum(former * latter), jnp.sum(former * former), jnp.sum(lat...]
    pallas_call x0 -> x1, Pallas kernels: none -> 90.2 us  [shards(): pl.pallas_call(kernel, out_shape=jax.ShapeDtypeStruct((rows, bw), F32), i...]
    ppermute x4 -> x0, waiting for transfers between devices: 90 us -> none  [partner_2(): lax.ppermute(x, axis, [(i, i ^ 1 << bit) for i in range(lax.axis_size(axi...]
    reduce_sum x4 -> x0, other arithmetic: 12.5 us -> none  [shards(): jnp.sum(former * former)]
    dot_general x1 -> x0, matrix products: 11.7 us -> none  [shards(): lax.dot_general(activations, out_grads, (((0,), (0,)), ((), ())), preferr...]
    ppermute x4 -> x0, starting transfers between devices: 8.08 us -> none  [partner_2(): lax.ppermute(x, axis, [(i, i ^ 1 << bit) for i in range(lax.axis_size(axi...]
    add x4 -> x0, other arithmetic: 5.54 us -> none  [shards(): (1.0 - inner_prod / (2.0 * (former_sq + epsilon))) * former]
  transfers between devices with their start and end apart: 5 -> 0, of which waited for: 5 -> 0; matrix products, arithmetic and copies ran while one was open for 0% -> 0% of each run, Pallas kernels for 0% -> 0%
where the time goes in v1:
time: 91.8 us; the launch traced here: 91.6 us
  Pallas kernels  90.2 us (98%)
  local copies, waits for them, and re-layouts  1.47 us (2%)
    pallas_call x1, Pallas kernels, shards(): pl.pallas_call(kernel, out_shape=jax.ShapeDtypeStruct((rows, bw), F32), i...  90.2 us

profile of v1, /device:TPU:1, one launch (start us, length us, event | category | flops | bytes accessed | tf_op | source)
XLA Modules:
  0.0 91.6 jit_solution(8573603901935753134)
XLA Ops:
  0.0 90.2 %adasum.1 = f32[32,512]{1,0:T(8,128)} custom-call(bf16[512,8192]{1,0:T(8,128)(2,1)} %a_hbm.1, bf16[512,512]{1,0:T(8,128)(2,1)} %g_hbm.1), custom_call_target="tpu_custom_call" | custom-call | flops 4294967296 | bytes 8912896 | tf_op jit(solution)/shard_map/adasum/pallas_call | solution.py:226
  90.2 1.5 %copy.4 = f32[512,32]{0,1:T(8,128)} copy(f32[512,32]{0,1:T(8,128)} %bitcast.1) | data formatting | bytes 131072

commit v2 on v1

v2 whole, which is shorter than its diff:
```python
import jax
import jax.numpy as jnp
from jax import lax
from jax.experimental import pallas as pl
from jax.experimental.pallas import tpu as pltpu
from jax.sharding import PartitionSpec as P

MESH = pl.DeviceIdType.MESH
EPS = 1e-6
NZ = 8
NG = 16
STEPS = NZ - 1
F32, BF16 = jnp.float32, jnp.bfloat16
SLOTS = (7, 1, 6, 2, 5, 3, 4, 0)


def kernel(
    a_hbm, g_hbm, out_ref,
    av, gv, gt, hs, hr, ls, lr, ts, tr, rest, xs, xr, zs, zr, ks, kz, kc,
    own_sem, par_send, par_recv, hi_send, hi_recv, lo_send, lo_recv, t_send, t_recv,
    x_send, x_recv, z_send, z_recv, k_send, k_recv, near_sem, far_sem,
):
    b = lax.axis_index("blk")
    g = lax.axis_index("cube")
    z, core = b >> 1, b & 1
    y, x = g >> 2, g & 3
    tok = a_hbm.shape[0]
    bw = a_hbm.shape[1] // (2 * NZ)
    half = bw // 2
    kv = g_hbm.shape[1]
    kvh = kv // 2
    ks_rows = kv // NG
    last = STEPS - 1

    def at_plane(dy, dx):
        return (((y + dy) & 3) * 4) + ((x + dx) & 3)

    partner = (b ^ 1, g)
    ring = ((((z + 1) & 7) * 2 + core, g), (((z + 7) & 7) * 2 + core, g))
    plane = [
        at_plane(dy, dx)
        for dy, dx in sorted(
            ((dy, dx) for dy in range(4) for dx in range(4) if dy or dx),
            key=lambda o: -(min(o[0], 4 - o[0]) + min(o[1], 4 - o[1])),
        )
    ]
    line = [(((z + dz) & 7) * 2 + core, g) for dz in (4, 3, 5, 2, 6, 1, 7)]
    beside = [(b, at_plane(dy, dx)) for dy, dx in ((0, 1), (0, 3), (1, 0), (3, 0))]
    across = [(b, at_plane(dy, dx)) for dy, dx in ((0, 2), (2, 0))]

    own = [pltpu.make_async_copy(g_hbm, gv, own_sem.at[NZ])]
    own[0].start()

    barrier = pltpu.get_barrier_semaphore()
    near = [partner, *ring, *beside]
    for p in near:
        pl.semaphore_signal(barrier, inc=1, device_id=p, device_id_type=MESH)

    def block(slot, parity):
        start = (((z + slot) & 7) * 2 + parity) * bw
        return a_hbm.at[:, pl.ds(pl.multiple_of(start, bw), bw)]

    for s in range(NZ):
        own.append(pltpu.make_async_copy(block(s, core), av.at[s, pl.ds(0, tok)], own_sem.at[s]))
    for s in SLOTS[:2]:
        own[s + 1].start()

    own[0].wait()
    gt[:, :tok] = gv[...].T
    pl.semaphore_wait(barrier, len(near))

    def remote(src, dst, send, recv, dev):
        return pltpu.make_async_remote_copy(
            src_ref=src, dst_ref=dst, send_sem=send, recv_sem=recv, device_id=dev, device_id_type=MESH
        )

    def par(slot, h):
        return remote(
            block(slot, 1 - core).at[:, pl.ds(h * half, half)],
            av.at[slot, pl.ds(tok, tok), pl.ds(h * half, half)],
            par_send.at[slot, h], par_recv.at[slot, h], partner,
        )

    def par_grad(way):
        rows = pl.ds(way * kvh, kvh)
        return remote(
            gt.at[rows, pl.ds(0, tok)], gt.at[rows, pl.ds(tok, tok)], par_send.at[NZ, way], par_recv.at[NZ, way], partner
        )

    for h in range(2):
        for way in range(2):
            if h == 0:
                par_grad(way).start()
            par(SLOTS[way], h).start()

    def fetch(slots):
        for s in slots:
            own[s + 1].start()
            for h in range(2):
                par(s, h).start()

    for p in beside:
        pl.semaphore_signal(near_sem, inc=1, device_id=p, device_id_type=MESH)

    waited = set()

    def ready(way, slot, h):
        if ("grad", way) not in waited:
            waited.add(("grad", way))
            par_grad(way).wait_recv()
        if slot not in waited:
            waited.add(slot)
            own[slot + 1].wait()
        if (slot, h) not in waited:
            waited.add((slot, h))
            par(slot, h).wait_recv()

    def share(slot, way, h):
        return jnp.dot(
            gt[way * kvh : (way + 1) * kvh, :],
            av[slot, :, h * half : (h + 1) * half],
            preferred_element_type=F32,
        )

    def hop(t, way, h):
        return remote(hs.at[t, way, h], hr.at[t, way, h], hi_send.at[t, way, h], hi_recv.at[t, way, h], ring[way])

    def trail(way, h):
        return remote(ts.at[way, h], tr.at[way, h], t_send.at[way, h], t_recv.at[way, h], ring[way])

    def parts(src, dst, send, recv):
        return [remote(src.at[p], dst.at[g], send, recv, (b, p)) for p in plane] + [
            pltpu.make_async_copy(src.at[g], dst.at[g], recv)
        ]

    def spread(src, dst, send, recv):
        for copy in parts(src, dst, send, recv):
            copy.start()

    def spread_wait_recv(dst, recv):
        pltpu.make_async_copy(dst, dst, recv).wait()

    def spread_wait_send(src, send):
        part = src.at[pl.ds(0, NG - 1)]
        pltpu.make_async_copy(part, part, send).wait()

    queue = []
    for t in range(STEPS + 1):
        for h in range(2):
            for way in range(2):
                if t == STEPS:
                    slot = 0
                else:
                    slot = NZ - 1 - t if way == 0 else 1 + t
                ready(way, slot, h)
                total = share(slot, way, h)
                if t > 0:
                    hop(t - 1, way, h).wait_recv()
                    total = total + hr[t - 1, way, h].astype(F32)
                hi = total.astype(BF16)
                if t < STEPS:
                    hs[t, way, h] = hi
                    hop(t, way, h).start()
                else:
                    xs[h, way * 8 : way * 8 + 8] = hi.reshape(8, ks_rows, half)
                lo = total - hi.astype(F32)
                if t < last:
                    ls[t, way * 8 : way * 8 + 8, :, h * half : (h + 1) * half] = lo.astype(BF16).reshape(8, ks_rows, half)
                elif t == last:
                    ts[way, h] = lo.astype(BF16)
                else:
                    rest[way, h] = lo
                for copy in queue[:4]:
                    copy.start()
                queue = queue[4:]
            if t == STEPS:
                spread(xs.at[h], xr.at[h], x_send.at[h], x_recv.at[h])
        fetch(SLOTS[2 * t + 2 : 2 * t + 4])
        if t == 0:
            pl.semaphore_wait(near_sem, len(beside))
            for p in across:
                pl.semaphore_signal(far_sem, inc=1, device_id=p, device_id_type=MESH)
            pl.semaphore_wait(far_sem, len(across))
        if t < last:
            queue = parts(ls.at[t], lr.at[t], lo_send.at[t], lo_recv.at[t])
        elif t == last:
            for h in range(2):
                for way in range(2):
                    trail(way, h).start()

    gram = None
    for h in range(2):
        spread_wait_recv(xr.at[h], x_recv.at[h])
        rows = xr[h].reshape(kv, half)
        part = lax.dot_general(rows, rows, (((1,), (1,)), ((), ())), preferred_element_type=F32)
        gram = part if gram is None else gram + part
    same = (lax.broadcasted_iota(jnp.int32, (kv, kv), 0) & (ks_rows - 1)) == (
        lax.broadcasted_iota(jnp.int32, (kv, kv), 1) & (ks_rows - 1)
    )
    gram = jnp.where(same, gram, 0.0).reshape(NG, ks_rows, kv).sum(axis=1)
    pick = (lax.broadcasted_iota(jnp.int32, (kv, 128), 0) >> 5) == lax.broadcasted_iota(jnp.int32, (kv, 128), 1)
    gram = jnp.dot(gram, pick.astype(F32), precision=lax.Precision.HIGHEST, preferred_element_type=F32)

    most = pl.ds(0, NG - 1)
    ks[0] = gram
    kc[g] = gram
    for p in plane:
        remote(ks.at[0], kc.at[g], k_send.at[0], k_recv.at[0], (b, p)).start()
    for h in range(2):
        for way in range(2):
            trail(way, h).wait_recv()
            lo = rest[way, h] + tr[way, h].astype(F32)
            ls[last, way * 8 : way * 8 + 8, :, h * half : (h + 1) * half] = lo.astype(BF16).reshape(8, ks_rows, half)
    pltpu.make_async_copy(kc.at[most], kc.at[most], k_recv.at[0]).wait()
    gram = kc[...].sum(axis=0)
    ks[1] = gram
    swap = remote(ks.at[1], kz.at[NZ], k_send.at[1], k_recv.at[1], partner)
    swap.start()
    swap.wait_recv()
    gram = gram + kz[NZ]
    ks[2] = gram
    kz[z] = gram
    for p in line:
        remote(ks.at[2], kz.at[z], k_send.at[2], k_recv.at[2], p).start()
    spread(ls.at[last], lr.at[last], lo_send.at[last], lo_recv.at[last])
    ahead = pl.ds(0, NZ - 1)
    pltpu.make_async_copy(kz.at[ahead], kz.at[ahead], k_recv.at[2]).wait()
    gram = kz[:NZ].sum(axis=0)

    row = lax.broadcasted_iota(jnp.int32, (NG, 128), 0)
    col = lax.broadcasted_iota(jnp.int32, (NG, 128), 1)
    coef = jnp.ones((NG, 1), F32)
    for level in range(4):
        bit = 1 << level
        diag = jnp.where(row == col, gram, 0.0)
        cross = jnp.where((row ^ bit) == col, gram, 0.0)

        def factor(axis):
            sq = jnp.maximum(jnp.sum(diag, axis=axis, keepdims=True), 0.0)
            return 1.0 - jnp.sum(cross, axis=axis, keepdims=True) / (2.0 * (sq + EPS))

        by_row, by_col = factor(1), factor(0)
        coef = coef * by_row
        gram = gram * by_row * by_col
        gram = gram + jnp.where((row & bit) != 0, pltpu.roll(gram, bit, 0), pltpu.roll(gram, NG - bit, 0))
        gram = gram + jnp.where((col & bit) != 0, pltpu.roll(gram, bit, 1), pltpu.roll(gram, 128 - bit, 1))
    coef = jnp.broadcast_to(coef, (NG, 128))

    def combine(ref):
        width = ref.shape[-1]
        acc = jnp.zeros((ks_rows, width), F32)
        for i in range(NG):
            acc = acc + jnp.tile(coef[i : i + 1], (1, width // 128)) * ref[i].astype(F32)
        return acc

    side = 2 * (g >> 3) - 1

    def home(t):
        dest = (z + (1 + t) * side + 8) & 7
        return remote(zs.at[t], zr.at[t], z_send.at[t], z_recv.at[t], (dest * 2 + core, g))

    for t in (3, 2, 4, 1, 5, 0):
        spread_wait_recv(lr.at[t], lo_recv.at[t])
        zs[t] = combine(lr.at[t]).astype(BF16)
        home(t).start()
    acc = jnp.concatenate([combine(xr.at[0]), combine(xr.at[1])], axis=1)
    spread_wait_recv(lr.at[last], lo_recv.at[last])
    acc = acc + combine(lr.at[last])
    for t in (0, 5, 1, 4, 2, 3):
        home(t).wait_recv()
        acc = acc + zr[t].astype(F32)
    out_ref[...] = acc

    for way in range(2):
        par_grad(way).wait_send()
        for h in range(2):
            for s in range(way * 4, way * 4 + 4):
                par(s, h).wait_send()
            for t in range(STEPS):
                hop(t, way, h).wait_send()
            trail(way, h).wait_send()
    for t in range(STEPS):
        spread_wait_send(ls.at[t], lo_send.at[t])
    for t in range(last):
        home(t).wait_send()
    for h in range(2):
        spread_wait_send(xs.at[h], x_send.at[h])
    pltpu.make_async_copy(kc.at[most], kc.at[most], k_send.at[0]).wait()
    swap.wait_send()
    pltpu.make_async_copy(kz.at[ahead], kz.at[ahead], k_send.at[2]).wait()


def shards(activations, out_grads):
    tok, d = activations.shape
    kv = out_grads.shape[1]
    bw = d // (2 * NZ)
    half = bw // 2
    rows = kv // NG
    dma = pltpu.SemaphoreType.DMA
    grad = pl.pallas_call(
        kernel,
        out_shape=jax.ShapeDtypeStruct((rows, bw), F32),
        in_specs=[pl.BlockSpec(memory_space=pl.ANY)] * 2,
        out_specs=pl.BlockSpec(memory_space=pltpu.VMEM),
        scratch_shapes=[
            pltpu.VMEM((NZ, 2 * tok, bw), BF16),
            pltpu.VMEM((tok, kv), BF16),
            pltpu.VMEM((kv, 2 * tok), BF16),
            pltpu.VMEM((STEPS, 2, 2, kv // 2, half), BF16),
            pltpu.VMEM((STEPS, 2, 2, kv // 2, half), BF16),
            pltpu.VMEM((STEPS, NG, rows, bw), BF16),
            pltpu.VMEM((STEPS, NG, rows, bw), BF16),
            pltpu.VMEM((2, 2, kv // 2, half), BF16),
            pltpu.VMEM((2, 2, kv // 2, half), BF16),
            pltpu.VMEM((2, 2, kv // 2, half), F32),
            pltpu.VMEM((2, NG, rows, half), BF16),
            pltpu.VMEM((2, NG, rows, half), BF16),
            pltpu.VMEM((STEPS - 1, rows, bw), BF16),
            pltpu.VMEM((STEPS - 1, rows, bw), BF16),
            pltpu.VMEM((3, NG, 128), F32),
            pltpu.VMEM((NZ + 1, NG, 128), F32),
            pltpu.VMEM((NG, NG, 128), F32),
            dma((NZ + 1,)),
            dma((NZ + 1, 2)),
            dma((NZ + 1, 2)),
            dma((STEPS, 2, 2)),
            dma((STEPS, 2, 2)),
            dma((STEPS,)),
            dma((STEPS,)),
            dma((2, 2)),
            dma((2, 2)),
            dma((2,)),
            dma((2,)),
            dma((STEPS - 1,)),
            dma((STEPS - 1,)),
            dma((3,)),
            dma((3,)),
            pltpu.SemaphoreType.REGULAR,
            pltpu.SemaphoreType.REGULAR,
        ],
        compiler_params=pltpu.CompilerParams(
            collective_id=0, has_side_effects=True, vmem_limit_bytes=56 << 20
        ),
        cost_estimate=pl.CostEstimate(
            flops=2 * tok * d * kv, bytes_accessed=2 * tok * (d + kv), transcendentals=0
        ),
        name="adasum",
    )(activations, out_grads)
    return grad.T


def solution(mesh):
    placed = (P(("blk", "cube"), None), P(("blk", "cube"), None))
    return jax.shard_map(
        shards, mesh=mesh, in_specs=placed, out_specs=P("blk", "cube"), check_vma=False
    )
```

time: 91.8 us -> 83.4 us (0.908)
  Pallas kernels: 90.2 us -> 81.8 us
    pallas_call x1, Pallas kernels: 90.2 us -> 81.8 us  [shards(): pl.pallas_call(kernel, out_shape=jax.ShapeDtypeStruct((rows, bw), F32), i...]
where the time goes in v2:
time: 83.4 us; the launch traced here: 83.3 us
  Pallas kernels  81.8 us (98%)
  local copies, waits for them, and re-layouts  1.47 us (2%)
    pallas_call x1, Pallas kernels, shards(): pl.pallas_call(kernel, out_shape=jax.ShapeDtypeStruct((rows, bw), F32), i...  81.8 us

profile of v2, /device:TPU:1, one launch (start us, length us, event | category | flops | bytes accessed | tf_op | source)
XLA Modules:
  0.0 83.3 jit_solution(14669205233978226748)
XLA Ops:
  0.0 81.8 %adasum.1 = f32[32,512]{1,0:T(8,128)} custom-call(bf16[512,8192]{1,0:T(8,128)(2,1)} %a_hbm.1, bf16[512,512]{1,0:T(8,128)(2,1)} %g_hbm.1), custom_call_target="tpu_custom_call" | custom-call | flops 4294967296 | bytes 8912896 | tf_op jit(solution)/shard_map/adasum/pallas_call | solution.py:300
  81.8 1.5 %copy.4 = f32[512,32]{0,1:T(8,128)} copy(f32[512,32]{0,1:T(8,128)} %bitcast.1) | data formatting | bytes 131072

commit v3 on v2

--- a/solution.py
+++ b/solution.py
@@ -11,14 +11,16 @@
 NG = 16
 STEPS = NZ - 1
 F32, BF16 = jnp.float32, jnp.bfloat16
-SLOTS = (7, 1, 6, 2, 5, 3, 4, 0)
+SLOTS = (7, 1, 6, 2, 0, 5, 3, 4)
+CHUNKS = ((0, 256), (256, 256))
+NC = len(CHUNKS)
 
 
 def kernel(
     a_hbm, g_hbm, out_ref,
-    av, gv, gt, hs, hr, ls, lr, ts, tr, rest, xs, xr, zs, zr, ks, kz, kc,
+    av, gv, gt, hs, hr, ls, lr, ts, tr, rest, ps, pr, rr, xs, xr, zs, zr, ks, kz, kc,
     own_sem, par_send, par_recv, hi_send, hi_recv, lo_send, lo_recv, t_send, t_recv,
-    x_send, x_recv, z_send, z_recv, k_send, k_recv, near_sem, far_sem,
+    p_send, p_recv, x_send, x_recv, z_send, z_recv, k_send, k_recv, near_sem, far_sem,
 ):
     b = lax.axis_index("blk")
     g = lax.axis_index("cube")
@@ -26,7 +28,6 @@
     y, x = g >> 2, g & 3
     tok = a_hbm.shape[0]
     bw = a_hbm.shape[1] // (2 * NZ)
-    half = bw // 2
     kv = g_hbm.shape[1]
     kvh = kv // 2
     ks_rows = kv // NG
@@ -74,10 +75,12 @@
             src_ref=src, dst_ref=dst, send_sem=send, recv_sem=recv, device_id=dev, device_id_type=MESH
         )
 
+    def cols(h):
+        return pl.ds(*CHUNKS[h])
+
     def par(slot, h):
         return remote(
-            block(slot, 1 - core).at[:, pl.ds(h * half, half)],
-            av.at[slot, pl.ds(tok, tok), pl.ds(h * half, half)],
+            block(slot, 1 - core).at[:, cols(h)], av.at[slot, pl.ds(tok, tok), cols(h)],
             par_send.at[slot, h], par_recv.at[slot, h], partner,
         )
 
@@ -87,16 +90,14 @@
             gt.at[rows, pl.ds(0, tok)], gt.at[rows, pl.ds(tok, tok)], par_send.at[NZ, way], par_recv.at[NZ, way], partner
         )
 
-    for h in range(2):
-        for way in range(2):
-            if h == 0:
-                par_grad(way).start()
-            par(SLOTS[way], h).start()
+    for way in range(2):
+        par_grad(way).start()
+        par(SLOTS[way], 0).start()
 
     def fetch(slots):
         for s in slots:
             own[s + 1].start()
-            for h in range(2):
+            for h in range(NC):
                 par(s, h).start()
 
     for p in beside:
@@ -118,24 +119,27 @@
     def share(slot, way, h):
         return jnp.dot(
             gt[way * kvh : (way + 1) * kvh, :],
-            av[slot, :, h * half : (h + 1) * half],
+            av[slot, :, cols(h)],
             preferred_element_type=F32,
         )
 
     def hop(t, way, h):
-        return remote(hs.at[t, way, h], hr.at[t, way, h], hi_send.at[t, way, h], hi_recv.at[t, way, h], ring[way])
-
-    def trail(way, h):
-        return remote(ts.at[way, h], tr.at[way, h], t_send.at[way, h], t_recv.at[way, h], ring[way])
+        return remote(
+            hs.at[t, way, :, cols(h)], hr.at[t, way, :, cols(h)], hi_send.at[t, way, h], hi_recv.at[t, way, h], ring[way]
+        )
+
+    def trail(way):
+        return remote(ts.at[way], tr.at[way], t_send.at[way], t_recv.at[way], ring[way])
 
     def parts(src, dst, send, recv):
         return [remote(src.at[p], dst.at[g], send, recv, (b, p)) for p in plane] + [
             pltpu.make_async_copy(src.at[g], dst.at[g], recv)
         ]
 
-    def spread(src, dst, send, recv):
-        for copy in parts(src, dst, send, recv):
-            copy.start()
+    def spread(src, dst, send, recv, part):
+        for p in plane:
+            remote(src.at[p, :, part], dst.at[g, :, part], send, recv, (b, p)).start()
+        pltpu.make_async_copy(src.at[g, :, part], dst.at[g, :, part], recv).start()
 
     def spread_wait_recv(dst, recv):
         pltpu.make_async_copy(dst, dst, recv).wait()
@@ -144,54 +148,70 @@
         part = src.at[pl.ds(0, NG - 1)]
         pltpu.make_async_copy(part, part, send).wait()
 
+    def slices(value, h):
+        return value.reshape(8, ks_rows, CHUNKS[h][1])
+
     queue = []
-    for t in range(STEPS + 1):
-        for h in range(2):
+    for t in range(STEPS):
+        for h in range(NC):
             for way in range(2):
-                if t == STEPS:
-                    slot = 0
-                else:
-                    slot = NZ - 1 - t if way == 0 else 1 + t
+                if t == 0 and h > 0:
+                    par(SLOTS[way], h).start()
+            for way in range(2):
+                slot = NZ - 1 - t if way == 0 else 1 + t
+                mine = slice(way * 8, way * 8 + 8)
                 ready(way, slot, h)
                 total = share(slot, way, h)
                 if t > 0:
                     hop(t - 1, way, h).wait_recv()
-                    total = total + hr[t - 1, way, h].astype(F32)
+                    total = total + hr[t - 1, way, :, cols(h)].astype(F32)
                 hi = total.astype(BF16)
-                if t < STEPS:
-                    hs[t, way, h] = hi
+                if t < last:
+                    hs[t, way, :, cols(h)] = hi
                     hop(t, way, h).start()
                 else:
-                    xs[h, way * 8 : way * 8 + 8] = hi.reshape(8, ks_rows, half)
-                lo = total - hi.astype(F32)
+                    xs[mine, :, cols(h)] = slices(hi, h)
+                    for p in range(way * 8, way * 8 + 8):
+                        remote(
+                            xs.at[p, :, cols(h)], xr.at[g, :, cols(h)], x_send.at[h], x_recv.at[h], (ring[way][0], p)
+                        ).start()
+                lo = (total - hi.astype(F32)).astype(BF16)
                 if t < last:
-                    ls[t, way * 8 : way * 8 + 8, :, h * half : (h + 1) * half] = lo.astype(BF16).reshape(8, ks_rows, half)
-                elif t == last:
-                    ts[way, h] = lo.astype(BF16)
+                    ls[t, mine, :, cols(h)] = slices(lo, h)
                 else:
-                    rest[way, h] = lo
-                for copy in queue[:4]:
+                    ts[way, :, cols(h)] = lo
+                for copy in queue[:5]:
                     copy.start()
-                queue = queue[4:]
-            if t == STEPS:
-                spread(xs.at[h], xr.at[h], x_send.at[h], x_recv.at[h])
-        fetch(SLOTS[2 * t + 2 : 2 * t + 4])
+                queue = queue[5:]
         if t == 0:
+            fetch(SLOTS[2:5])
             pl.semaphore_wait(near_sem, len(beside))
             for p in across:
                 pl.semaphore_signal(far_sem, inc=1, device_id=p, device_id_type=MESH)
             pl.semaphore_wait(far_sem, len(across))
-        if t < last:
-            queue = parts(ls.at[t], lr.at[t], lo_send.at[t], lo_recv.at[t])
+        elif t == 1:
+            fetch(SLOTS[5:])
+            for h in range(NC):
+                for way in range(2):
+                    ready(way, 0, h)
+                    total = share(0, way, h)
+                    hi = total.astype(BF16)
+                    ps[way * 8 : way * 8 + 8, :, cols(h)] = slices(hi, h)
+                    rest[way, :, cols(h)] = total - hi.astype(F32)
+            queue = queue + parts(ps, pr, p_send.at[0], p_recv.at[0])
+        if t < last - 1:
+            queue = queue + parts(ls.at[t], lr.at[t], lo_send.at[t], lo_recv.at[t])
         elif t == last:
-            for h in range(2):
-                for way in range(2):
-                    trail(way, h).start()
+            for way in range(2):
+                trail(way).start()
 
     gram = None
-    for h in range(2):
-        spread_wait_recv(xr.at[h], x_recv.at[h])
-        rows = xr[h].reshape(kv, half)
+    spread_wait_recv(pr, p_recv.at[0])
+    for h in range(NC):
+        spread_wait_recv(xr.at[:, :, cols(h)], x_recv.at[h])
+        whole = xr[:, :, cols(h)].astype(F32) + pr[:, :, cols(h)].astype(F32)
+        rr[:, :, cols(h)] = whole
+        rows = whole.astype(BF16).reshape(kv, CHUNKS[h][1])
         part = lax.dot_general(rows, rows, (((1,), (1,)), ((), ())), preferred_element_type=F32)
         gram = part if gram is None else gram + part
     same = (lax.broadcasted_iota(jnp.int32, (kv, kv), 0) & (ks_rows - 1)) == (
@@ -206,23 +226,24 @@
     kc[g] = gram
     for p in plane:
         remote(ks.at[0], kc.at[g], k_send.at[0], k_recv.at[0], (b, p)).start()
-    for h in range(2):
-        for way in range(2):
-            trail(way, h).wait_recv()
-            lo = rest[way, h] + tr[way, h].astype(F32)
-            ls[last, way * 8 : way * 8 + 8, :, h * half : (h + 1) * half] = lo.astype(BF16).reshape(8, ks_rows, half)
+    for way in range(2):
+        trail(way).wait_recv()
+        lo = rest[way] + tr[way].astype(F32)
+        ls[last, way * 8 : way * 8 + 8] = lo.astype(BF16).reshape(8, ks_rows, bw)
     pltpu.make_async_copy(kc.at[most], kc.at[most], k_recv.at[0]).wait()
     gram = kc[...].sum(axis=0)
     ks[1] = gram
     swap = remote(ks.at[1], kz.at[NZ], k_send.at[1], k_recv.at[1], partner)
     swap.start()
+    late = last - 1
+    spread(ls.at[late], lr.at[late], lo_send.at[late], lo_recv.at[late], slice(None))
     swap.wait_recv()
     gram = gram + kz[NZ]
     ks[2] = gram
     kz[z] = gram
     for p in line:
         remote(ks.at[2], kz.at[z], k_send.at[2], k_recv.at[2], p).start()
-    spread(ls.at[last], lr.at[last], lo_send.at[last], lo_recv.at[last])
+    spread(ls.at[last], lr.at[last], lo_send.at[last], lo_recv.at[last], slice(None))
     ahead = pl.ds(0, NZ - 1)
     pltpu.make_async_copy(kz.at[ahead], kz.at[ahead], k_recv.at[2]).wait()
     gram = kz[:NZ].sum(axis=0)
@@ -263,38 +284,39 @@
         spread_wait_recv(lr.at[t], lo_recv.at[t])
         zs[t] = combine(lr.at[t]).astype(BF16)
         home(t).start()
-    acc = jnp.concatenate([combine(xr.at[0]), combine(xr.at[1])], axis=1)
+    acc = combine(rr)
+    for way in range(2):
+        par_grad(way).wait_send()
+        trail(way).wait_send()
+        for t in range(last):
+            for h in range(NC):
+                hop(t, way, h).wait_send()
+    for s in range(NZ):
+        for h in range(NC):
+            par(s, h).wait_send()
+    for t in range(STEPS):
+        spread_wait_send(ls.at[t], lo_send.at[t])
+    for h in range(NC):
+        sent = xs.at[:, :, cols(h)]
+        pltpu.make_async_copy(sent, sent, x_send.at[h]).wait()
+    spread_wait_send(ps, p_send.at[0])
+    pltpu.make_async_copy(kc.at[most], kc.at[most], k_send.at[0]).wait()
+    swap.wait_send()
+    pltpu.make_async_copy(kz.at[ahead], kz.at[ahead], k_send.at[2]).wait()
     spread_wait_recv(lr.at[last], lo_recv.at[last])
     acc = acc + combine(lr.at[last])
     for t in (0, 5, 1, 4, 2, 3):
         home(t).wait_recv()
         acc = acc + zr[t].astype(F32)
     out_ref[...] = acc
-
-    for way in range(2):
-        par_grad(way).wait_send()
-        for h in range(2):
-            for s in range(way * 4, way * 4 + 4):
-                par(s, h).wait_send()
-            for t in range(STEPS):
-                hop(t, way, h).wait_send()
-            trail(way, h).wait_send()
-    for t in range(STEPS):
-        spread_wait_send(ls.at[t], lo_send.at[t])
     for t in range(last):
         home(t).wait_send()
-    for h in range(2):
-        spread_wait_send(xs.at[h], x_send.at[h])
-    pltpu.make_async_copy(kc.at[most], kc.at[most], k_send.at[0]).wait()
-    swap.wait_send()
-    pltpu.make_async_copy(kz.at[ahead], kz.at[ahead], k_send.at[2]).wait()
 
 
 def shards(activations, out_grads):
     tok, d = activations.shape
     kv = out_grads.shape[1]
     bw = d // (2 * NZ)
-    half = bw // 2
     rows = kv // NG
     dma = pltpu.SemaphoreType.DMA
     grad = pl.pallas_call(
@@ -306,15 +328,18 @@
             pltpu.VMEM((NZ, 2 * tok, bw), BF16),
             pltpu.VMEM((tok, kv), BF16),
             pltpu.VMEM((kv, 2 * tok), BF16),
-            pltpu.VMEM((STEPS, 2, 2, kv // 2, half), BF16),
-            pltpu.VMEM((STEPS, 2, 2, kv // 2, half), BF16),
+            pltpu.VMEM((STEPS - 1, 2, kv // 2, bw), BF16),
+            pltpu.VMEM((STEPS - 1, 2, kv // 2, bw), BF16),
             pltpu.VMEM((STEPS, NG, rows, bw), BF16),
             pltpu.VMEM((STEPS, NG, rows, bw), BF16),
-            pltpu.VMEM((2, 2, kv // 2, half), BF16),
-            pltpu.VMEM((2, 2, kv // 2, half), BF16),
-            pltpu.VMEM((2, 2, kv // 2, half), F32),
-            pltpu.VMEM((2, NG, rows, half), BF16),
-            pltpu.VMEM((2, NG, rows, half), BF16),
+            pltpu.VMEM((2, kv // 2, bw), BF16),
+            pltpu.VMEM((2, kv // 2, bw), BF16),
+            pltpu.VMEM((2, kv // 2, bw), F32),
+            pltpu.VMEM((NG, rows, bw), BF16),
+            pltpu.VMEM((NG, rows, bw), BF16),
+            pltpu.VMEM((NG, rows, bw), F32),
+            pltpu.VMEM((NG, rows, bw), BF16),
+            pltpu.VMEM((NG, rows, bw), BF16),
             pltpu.VMEM((STEPS - 1, rows, bw), BF16),
             pltpu.VMEM((STEPS - 1, rows, bw), BF16),
             pltpu.VMEM((3, NG, 128), F32),
@@ -323,14 +348,16 @@
             dma((NZ + 1,)),
             dma((NZ + 1, 2)),
             dma((NZ + 1, 2)),
-            dma((STEPS, 2, 2)),
-            dma((STEPS, 2, 2)),
+            dma((STEPS - 1, 2, NC)),
+            dma((STEPS - 1, 2, NC)),
             dma((STEPS,)),
             dma((STEPS,)),
-            dma((2, 2)),
-            dma((2, 2)),
             dma((2,)),
             dma((2,)),
+            dma((1,)),
+            dma((1,)),
+            dma((NC,)),
+            dma((NC,)),
             dma((STEPS - 1,)),
             dma((STEPS - 1,)),
             dma((3,)),

time: 83.4 us -> 82.3 us (0.987)
  Pallas kernels: 81.8 us -> 80.6 us
    pallas_call x1, Pallas kernels: 81.8 us -> 80.6 us  [shards(): pl.pallas_call(kernel, out_shape=jax.ShapeDtypeStruct((rows, bw), F32), i...]
where the time goes in v3:
time: 82.3 us; the launch traced here: 82.1 us
  Pallas kernels  80.6 us (98%)
  local copies, waits for them, and re-layouts  1.47 us (2%)
    pallas_call x1, Pallas kernels, shards(): pl.pallas_call(kernel, out_shape=jax.ShapeDtypeStruct((rows, bw), F32), i...  80.6 us

profile of v3, /device:TPU:1, one launch (start us, length us, event | category | flops | bytes accessed | tf_op | source)
XLA Modules:
  0.0 82.1 jit_solution(10136322762700456250)
XLA Ops:
  0.0 80.6 %adasum.1 = f32[32,512]{1,0:T(8,128)} custom-call(bf16[512,8192]{1,0:T(8,128)(2,1)} %a_hbm.1, bf16[512,512]{1,0:T(8,128)(2,1)} %g_hbm.1), custom_call_target="tpu_custom_call" | custom-call | flops 4294967296 | bytes 8912896 | tf_op jit(solution)/shard_map/adasum/pallas_call | solution.py:322
  80.6 1.5 %copy.4 = f32[512,32]{0,1:T(8,128)} copy(f32[512,32]{0,1:T(8,128)} %bitcast.1) | data formatting | bytes 131072

commit v4 on v3

--- a/solution.py
+++ b/solution.py
@@ -201,9 +201,6 @@
             queue = queue + parts(ps, pr, p_send.at[0], p_recv.at[0])
         if t < last - 1:
             queue = queue + parts(ls.at[t], lr.at[t], lo_send.at[t], lo_recv.at[t])
-        elif t == last:
-            for way in range(2):
-                trail(way).start()
 
     gram = None
     spread_wait_recv(pr, p_recv.at[0])
@@ -227,22 +224,24 @@
     for p in plane:
         remote(ks.at[0], kc.at[g], k_send.at[0], k_recv.at[0], (b, p)).start()
     for way in range(2):
-        trail(way).wait_recv()
-        lo = rest[way] + tr[way].astype(F32)
-        ls[last, way * 8 : way * 8 + 8] = lo.astype(BF16).reshape(8, ks_rows, bw)
+        trail(way).start()
     pltpu.make_async_copy(kc.at[most], kc.at[most], k_recv.at[0]).wait()
     gram = kc[...].sum(axis=0)
     ks[1] = gram
     swap = remote(ks.at[1], kz.at[NZ], k_send.at[1], k_recv.at[1], partner)
     swap.start()
-    late = last - 1
-    spread(ls.at[late], lr.at[late], lo_send.at[late], lo_recv.at[late], slice(None))
     swap.wait_recv()
     gram = gram + kz[NZ]
     ks[2] = gram
     kz[z] = gram
     for p in line:
         remote(ks.at[2], kz.at[z], k_send.at[2], k_recv.at[2], p).start()
+    late = last - 1
+    spread(ls.at[late], lr.at[late], lo_send.at[late], lo_recv.at[late], slice(None))
+    for way in range(2):
+        trail(way).wait_recv()
+        lo = rest[way] + tr[way].astype(F32)
+        ls[last, way * 8 : way * 8 + 8] = lo.astype(BF16).reshape(8, ks_rows, bw)
     spread(ls.at[last], lr.at[last], lo_send.at[last], lo_recv.at[last], slice(None))
     ahead = pl.ds(0, NZ - 1)
     pltpu.make_async_copy(kz.at[ahead], kz.at[ahead], k_recv.at[2]).wait()
@@ -280,7 +279,7 @@
         dest = (z + (1 + t) * side + 8) & 7
         return remote(zs.at[t], zr.at[t], z_send.at[t], z_recv.at[t], (dest * 2 + core, g))
 
-    for t in (3, 2, 4, 1, 5, 0):
+    for t in (3, 2, 4, 1, 0, 5):
         spread_wait_recv(lr.at[t], lo_recv.at[t])
         zs[t] = combine(lr.at[t]).astype(BF16)
         home(t).start()

time: 82.3 us -> 81.3 us (0.988)
  Pallas kernels: 80.6 us -> 79.7 us
    pallas_call x1, Pallas kernels: 80.6 us -> 79.7 us  [shards(): pl.pallas_call(kernel, out_shape=jax.ShapeDtypeStruct((rows, bw), F32), i...]
where the time goes in v4:
time: 81.3 us; the launch traced here: 81.1 us
  Pallas kernels  79.7 us (98%)
  local copies, waits for them, and re-layouts  1.47 us (2%)
    pallas_call x1, Pallas kernels, shards(): pl.pallas_call(kernel, out_shape=jax.ShapeDtypeStruct((rows, bw), F32), i...  79.7 us

profile of v4, /device:TPU:1, one launch (start us, length us, event | category | flops | bytes accessed | tf_op | source)
XLA Modules:
  0.0 81.1 jit_solution(10839029286769653849)
XLA Ops:
  0.0 79.7 %adasum.1 = f32[32,512]{1,0:T(8,128)} custom-call(bf16[512,8192]{1,0:T(8,128)(2,1)} %a_hbm.1, bf16[512,512]{1,0:T(8,128)(2,1)} %g_hbm.1), custom_call_target="tpu_custom_call" | custom-call | flops 4294967296 | bytes 8912896 | tf_op jit(solution)/shard_map/adasum/pallas_call | solution.py:321
  79.7 1.5 %copy.4 = f32[512,32]{0,1:T(8,128)} copy(f32[512,32]{0,1:T(8,128)} %bitcast.1) | data formatting | bytes 131072

commit v5 on v4

--- a/solution.py
+++ b/solution.py
@@ -171,7 +171,8 @@
                     hop(t, way, h).start()
                 else:
                     xs[mine, :, cols(h)] = slices(hi, h)
-                    for p in range(way * 8, way * 8 + 8):
+                    for i in range(8):
+                        p = way * 8 + ((g + i) & 7)
                         remote(
                             xs.at[p, :, cols(h)], xr.at[g, :, cols(h)], x_send.at[h], x_recv.at[h], (ring[way][0], p)
                         ).start()

time: 81.3 us -> 81.3 us (level)
  no operation moved by 1% of the time
where the time goes in v5:
time: 81.3 us; the launch traced here: 80.5 us
  Pallas kernels  79 us (97%)
  local copies, waits for them, and re-layouts  1.47 us (2%)
    pallas_call x1, Pallas kernels, shards(): pl.pallas_call(kernel, out_shape=jax.ShapeDtypeStruct((rows, bw), F32), i...  79 us

profile of v5, /device:TPU:1, one launch (start us, length us, event | category | flops | bytes accessed | tf_op | source)
XLA Modules:
  0.0 80.5 jit_solution(2145204073251959617)
XLA Ops:
  0.0 79.0 %adasum.1 = f32[32,512]{1,0:T(8,128)} custom-call(bf16[512,8192]{1,0:T(8,128)(2,1)} %a_hbm.1, bf16[512,512]{1,0:T(8,128)(2,1)} %g_hbm.1), custom_call_target="tpu_custom_call" | custom-call | flops 4294967296 | bytes 8912896 | tf_op jit(solution)/shard_map/adasum/pallas_call | solution.py:322
  79.0 1.5 %copy.4 = f32[512,32]{0,1:T(8,128)} copy(f32[512,32]{0,1:T(8,128)} %bitcast.1) | data formatting | bytes 131072
